TPU v7x, 512 devices: a whole 4x4x16 slice. The times are simulated.
512 devices in a mesh: role: 2 (over y_lo), ep: 128 (over z, x, core), tp: 2 (over y_hi).
Axes of the slice: x: 4, y: 4 (y_hi: 2, y_lo: 2; y = y_hi * 2 + y_lo), z: 16, core: 2. Of those that a mesh axis runs over, the one named last changes fastest.
Arguments:
- routes: int32 [4096, 8], P(('role', 'ep')), may hold values from 0 to 127, all different within a row; in each aligned block of 16 rows (0 to 15, 16 to 31, ...) at most 2 rows name the same one
- gate_weights: float32 [4096, 8], P(('role', 'ep')), may hold values from 0.05 to 0.5
- expert_hidden: bfloat16 [256, 256, 1024], P(('role', 'ep'), None, 'tp'), may hold values from -6 to 6
- down_weight: bfloat16 [128, 1024, 3584], P('ep', None, 'tp'), may hold values from -0.1875 to 0.1875
- queries: bfloat16 [256, 2, 2, 128, 576], P(('role', 'ep'), None, None, 'tp'), may hold values from -4 to 4
- new_latents: bfloat16 [256, 2, 2, 576], P(('role', 'ep')), may hold values from -4 to 4
- lengths: int32 [256], replicated, may hold values from 128 to 1024
- destinations: int32 [128], replicated, may hold values from 0 to 127, as said below
- latent_cache: bfloat16 [256, 1024, 576], P(('role', 'ep'), 'tp'), may hold values from -4 to 4
Outputs:
- moe_output: bfloat16 [4096, 3584], P(('role', 'ep'), 'tp')
- attention_output: bfloat16 [256, 2, 2, 128, 512], P(('role', 'ep'), None, None, 'tp')
Inputs may be any that keep to these rules, and one draw needn't show every extreme that they name: `routes`: in each aligned block of 16 rows no expert is named more than 2 times. destinations[i] is i or i XOR 1, and destinations[destinations[i]] = i.
All inputs are finite; a program needn't handle non-finite values.
Results may differ from a plain program's by a relative error of at most 0.0049.
Values may be sent and summed in bfloat16 or wider, within the bound.
A program may use at most 64 MiB of HBM per device.

v0:
```python
import jax
import jax.numpy as jnp
from jax import lax
from jax.sharding import PartitionSpec as P

VLAT = 512


SCORE_SCALE = 0.07216878364870322
VERY_LOW = -1e30


def passed_along(value, axis, by):
    count = lax.axis_size(axis)
    pairs = [(i, i + by) for i in range(count) if 0 <= i + by < count]
    return lax.ppermute(value, axis, pairs)


def swapped(value, axis, apart):
    return lax.ppermute(value, axis, [(i, i ^ 1 << apart) for i in range(lax.axis_size(axis))])


def slot_numbers(pick_table):
    flat_picks = pick_table.reshape(-1)
    pick_count = flat_picks.shape[0]
    same_pick = (flat_picks[:, None] == flat_picks[None, :]).astype(jnp.int32)
    earlier = (
        lax.broadcasted_iota(jnp.int32, (pick_count, pick_count), 1)
        < lax.broadcasted_iota(jnp.int32, (pick_count, pick_count), 0)
    ).astype(jnp.int32)
    return jnp.sum(same_pick * earlier, axis=1).reshape(pick_table.shape)


def local(
    routes,
    gate_weights,
    expert_hidden,
    down_weight,
    queries,
    new_latents,
    lengths,
    destinations,
    latent_cache,
):
    sources = lax.axis_size("ep")
    capacity = expert_hidden.shape[1] // sources
    local_experts = expert_hidden.shape[0]
    width_half = down_weight.shape[2]
    expert_sum = jnp.einsum(
        "erh,ehd->erd",
        lax.all_gather(expert_hidden, "tp", axis=2, tiled=True),
        down_weight,
        preferred_element_type=jnp.float32,
    )
    sent_rows = expert_sum.astype(jnp.bfloat16).reshape(
        local_experts, sources, capacity, width_half
    )
    returned = lax.all_to_all(sent_rows, "ep", split_axis=1, concat_axis=0, tiled=True).reshape(
        -1, width_half
    )
    slot_index = slot_numbers(routes)
    row_index = routes * capacity + slot_index
    picked = returned[row_index]
    moe_output = jnp.sum(gate_weights[:, :, None] * picked.astype(jnp.float32), axis=1).astype(
        jnp.bfloat16
    )
    ep_index = lax.axis_index("ep")
    role_index = lax.axis_index("role")
    decoding = role_index > 0
    own_row = role_index * sources + ep_index
    own_shard = latent_cache[0]
    own_span = new_latents[0].reshape(-1, new_latents.shape[3])
    shard_len = own_shard.shape[0]
    span_len = own_span.shape[0]
    package = jnp.concatenate([own_shard, own_span], axis=0)
    paired = destinations[ep_index]
    flipped = paired != ep_index
    carried = passed_along(package, "role", 1)
    partner = swapped(carried, "ep", 0)
    arrived = jnp.where(flipped, partner, carried)
    second_shard = jnp.where(decoding, arrived[:shard_len], own_shard)
    second_span = jnp.where(decoding, arrived[shard_len:], own_span)
    second_len = jnp.where(decoding, lengths[paired], lengths[own_row])
    group_lengths = jnp.stack([lengths[own_row], second_len])
    group_caches = jnp.stack([own_shard, second_shard])
    query_set = queries[0]
    steps_here = query_set.shape[1]
    counts_now = jnp.stack(
        [jnp.zeros((), jnp.int32), jnp.where(decoding, span_len, steps_here).astype(jnp.int32)]
    )
    extra_keys = jnp.concatenate([jnp.stack([own_span, second_span]), new_latents[0]], axis=1)
    extra_scores = (
        jnp.einsum("gshl,gel->gshe", query_set, extra_keys, preferred_element_type=jnp.float32)
        * SCORE_SCALE
    )
    key_ids = lax.broadcasted_iota(jnp.int32, (1, 1, extra_keys.shape[1]), 2)
    step_ids = lax.broadcasted_iota(jnp.int32, (1, steps_here, 1), 1)
    prior_ok = key_ids < counts_now[:, None, None]
    own_ok = key_ids - span_len <= step_ids
    extra_ok = jnp.where(key_ids < span_len, prior_ok, own_ok)[:, :, None, :]
    kept_scores = jnp.where(extra_ok, extra_scores, VERY_LOW)
    row_top = jnp.max(kept_scores, axis=3)
    extra_weights = jnp.where(extra_ok, jnp.exp(kept_scores - row_top[..., None]), 0.0)
    extra_sum = jnp.sum(extra_weights, axis=3)
    extra_values = extra_keys[..., :VLAT].astype(jnp.float32)
    extra_weighted = jnp.einsum(
        "gshe,gev->gshv", extra_weights, extra_values, precision=lax.Precision.HIGHEST
    )
    shard_rows = lax.all_gather(group_caches, "tp", axis=1, tiled=True)
    positions = lax.broadcasted_iota(jnp.int32, (1, shard_rows.shape[1]), 1)
    visible = (positions < group_lengths[:, None])[:, None, None, :]
    scores = (
        jnp.einsum("gshl,gpl->gshp", query_set, shard_rows, preferred_element_type=jnp.float32)
        * SCORE_SCALE
    )
    masked_scores = jnp.where(visible, scores, VERY_LOW)
    fresh_top = jnp.maximum(row_top, jnp.max(masked_scores, axis=3))
    factor = jnp.exp(row_top - fresh_top)
    piece_weights = jnp.where(visible, jnp.exp(masked_scores - fresh_top[..., None]), 0.0)
    fresh_sum = factor * extra_sum + jnp.sum(piece_weights, axis=3)
    piece_values = shard_rows[..., :VLAT].astype(jnp.float32)
    fresh_weighted = factor[..., None] * extra_weighted + jnp.einsum(
        "gshp,gpv->gshv", piece_weights, piece_values, precision=lax.Precision.HIGHEST
    )
    attention_output = (fresh_weighted / fresh_sum[..., None]).astype(jnp.bfloat16)[None]
    return (moe_output, attention_output)


def solution(mesh):
    placed = (
        P(("role", "ep"), None),
        P(("role", "ep"), None),
        P(("role", "ep"), None, "tp"),
        P("ep", None, "tp"),
        P(("role", "ep"), None, None, "tp", None),
        P(("role", "ep"), None, None, None),
        P(),
        P(),
        P(("role", "ep"), "tp", None),
    )
    return jax.shard_map(
        local,
        mesh=mesh,
        in_specs=placed,
        out_specs=(P(("role", "ep"), "tp"), P(("role", "ep"), None, None, "tp", None)),
        check_vma=False,
    )
```

profile of v0, /device:TPU:57, one launch (start us, length us, event | category | flops | bytes accessed | tf_op | source)
XLA Modules:
  0.0 127.4 jit_solution(9735673057106640379)
XLA Ops:
  7.2 1.4 %copy.34 = bf16[1,512,576]{2,1,0:T(8,128)(2,1)S(1)} copy(bf16[1,512,576]{1,2,0:T(8,128)(2,1)} %param.17) | data formatting | bytes 1179648 | tf_op args[8]
  8.7 0.7 reshape_squeeze.3
  9.4 1.3 %collective-permute-start = (bf16[516,576]{1,0:T(8,128)(2,1)S(1)}, bf16[516,576]{1,0:T(8,128)(2,1)S(1)}, u32[]{:S(2)}, u32[]{:S(2)}) collective-permute-start(bf16[516,576]{1,0:T(8,128)(2,1)S(1)} %pad_maximum_fusion.1), channel_id=1, source_target_pairs={{0,256},{1,257},{2,258},{3,259},{4,260},{5,261},{6,262},{7,263},{8... | collective-permute-start | bytes 1783304 | tf_op jit(solution)/shard_map/ppermute | solution.py:16
  10.7 16.4 %collective-permute-done = bf16[516,576]{1,0:T(8,128)(2,1)S(1)} collective-permute-done((bf16[516,576]{1,0:T(8,128)(2,1)S(1)}, bf16[516,576]{1,0:T(8,128)(2,1)S(1)}, u32[]{:S(2)}, u32[]{:S(2)}) %collective-permute-start) | collective-permute-done | bytes 594464 | tf_op jit(solution)/shard_map/ppermute | solution.py:16
  27.2 3.4 %collective-permute-start.1 = (bf16[516,576]{1,0:T(8,128)(2,1)S(1)}, bf16[516,576]{1,0:T(8,128)(2,1)S(1)}, u32[]{:S(2)}, u32[]{:S(2)}) collective-permute-start(bf16[516,576]{1,0:T(8,128)(2,1)S(1)} %collective-permute-done), channel_id=1, source_target_pairs={{0,2},{2,0},{4,6},{6,4},{8,10},{10,8},{12,14},{14,12},{16,18},{18,... | collective-permute-start | bytes 1783304 | tf_op jit(solution)/shard_map/ppermute | solution.py:20
  30.6 1.2 dynamic_slice.10
  32.5 10.2 %all_gather.6 = bf16[1,256,1024]{2,1,0:T(8,128)(2,1)} all-gather(bf16[1,256,512]{2,1,0:T(8,128)(2,1)S(1)} %copy-done.3), channel_id=1, replica_groups=mesh['role'=2,'ep'=128,'tp'=2] {'tp'}, dimensions={2}, use_global_device_ids=true | all-gather | bytes 786432 | tf_op jit(solution)/shard_map/all_gather | solution.py:51
  42.9 1.3 pad_maximum_fusion
  44.3 3.2 %fusion.4 = bf16[256,1792]{1,0:T(8,128)(2,1)S(1)} fusion(bf16[1,1024,1792]{2,1,0:T(8,128)(2,1)} %param.12, bf16[1,256,1024]{2,1,0:T(8,128)(2,1)S(1)} %copy-done.2), kind=kOutput, calls=%fused_computation.5 | convolution fusion | flops 939982848 | bytes 5111808 | tf_op jit(solution)/shard_map/erh,ehd->erd/dot_general | solution.py:49
  47.5 1.3 %reshape.126 = bf16[1,128,2,1792]{3,2,1,0:T(2,128)(2,1)} reshape(bf16[256,1792]{1,0:T(8,128)(2,1)S(1)} %fusion.4) | data formatting | bytes 1835008 | tf_op jit(solution)/shard_map/reshape | solution.py:55
  48.8 19.4 %all-to-all-start = ((bf16[1,128,2,1792]{3,2,0,1:T(2,128)(2,1)}), bf16[1,128,2,1792]{3,2,0,1:T(2,128)(2,1)S(1)}, u32[]{:S(2)}, u32[]{:S(2)}) async-start(bf16[1,128,2,1792]{3,2,0,1:T(2,128)(2,1)} %bitcast.2), calls=%async_computation | async-start | bytes 1835008 | tf_op jit(solution)/shard_map/all_to_all | solution.py:58
  69.7 0.2 select_reduce_fusion
  70.8 0.6 fusion.40
  72.8 0.7 pad_add_fusion.1
  73.8 0.3 fusion.41
  74.1 23.2 %all-gather.2.cloned.1.call-done = bf16[2,1024,576]{2,1,0:T(8,128)(2,1)} async-done(((bf16[2,512,576]{2,1,0:T(8,128)(2,1)}), bf16[2,1024,576]{2,1,0:T(8,128)(2,1)}) %all-gather.2.cloned.1.call-update) | async-done | bytes 2359312 | tf_op jit(solution)/shard_map/all_gather | solution.py:109
  97.4 2.9 %fusion.42 = (f32[2,2,64]{2,1,0:T(2,128)S(1)}, f32[2,2,64,1024]{3,2,1,0:T(8,128)S(1)}) fusion(bf16[1,2,2,64,576]{4,3,2,1,0:T(8,128)(2,1)S(1)} %copy-done, bf16[2,1024,576]{2,1,0:T(8,128)(2,1)} %all-gather.2.cloned.1.call-done, pred[2,1024]{1,0:T(4,128)(4,1)S(1)} %iota_compare_fusion.1), kind=kOutput, calls=%fused_computation.62 | convolution fusion | flops 302776064 | bytes 3705856 | tf_op jit(solution)/shard_map/gshl,gpl->gshp/dot_general | solution.py:113
  100.3 0.3 fusion.24
  100.6 0.5 convolution_multiply_fusion
  101.2 1.9 %fusion.20 = bf16[1,2,2,64,512]{4,3,2,1,0:T(8,128)(2,1)} fusion(f32[2,2,64,512]{3,2,1,0:T(8,128)S(1)} %convolution_multiply_fusion, bf16[2,1024,576]{2,1,0:T(8,128)(2,1)S(1)} %copy-done.1, f32[2,2,64,1024]{3,2,1,0:T(8,128)S(1)} %get-tuple-element.9, f32[2,2,64]{2,1,0:T(2,128)S(1)} %max.13, pred[2,1024]{1,0:T(4,128)(4,1)S(1)} %iota_compare_fusion.1, ...), kind=kOutput, calls=%fused_computation.16 | convolution fusion | flops 1611530240 | bytes 3940352 | tf_op jit(solution)/shard_map/gshp,gpv->gshv/dot_general | solution.py:122
  103.1 15.2 %all-to-all-done = bf16[1,128,2,1792]{3,2,0,1:T(2,128)(2,1)S(1)} async-done(((bf16[1,128,2,1792]{3,2,0,1:T(2,128)(2,1)}), bf16[1,128,2,1792]{3,2,0,1:T(2,128)(2,1)S(1)}, u32[]{:S(2)}, u32[]{:S(2)}) %all-to-all-start) | async-done | bytes 917536 | tf_op jit(solution)/shard_map/all_to_all | solution.py:58
  118.3 0.3 reshape.127
  118.6 0.9 gather_fusion
  119.5 1.1 fusion.23
  (41 shorter events, 1.2 us)
Async XLA Ops:
  7.2 66.6 %copy-start = (bf16[1,2,2,64,576]{4,3,2,1,0:T(8,128)(2,1)S(1)}, bf16[1,2,2,64,576]{4,3,2,1,0:T(8,128)(2,1)}, u32[]{:S(2)}) copy-start(bf16[1,2,2,64,576]{4,3,2,1,0:T(8,128)(2,1)} %param.13) | copy-start | bytes 884740
  7.2 25.3 %copy-start.3 = (bf16[1,256,512]{2,1,0:T(8,128)(2,1)S(1)}, bf16[1,256,512]{2,1,0:T(8,128)(2,1)}, u32[]{:S(2)}) copy-start(bf16[1,256,512]{2,1,0:T(8,128)(2,1)} %param.11) | copy-start | bytes 786436
  7.2 90.2 %all-gather.2.cloned.1.call-start = ((), (), s32[]{:S(2)}) async-start(), calls=%async_computation.1 | async-start | bytes 3932160 | tf_op jit(solution)/shard_map/all_gather | solution.py:109
  9.4 17.7 %collective-permute-start = (bf16[516,576]{1,0:T(8,128)(2,1)S(1)}, bf16[516,576]{1,0:T(8,128)(2,1)S(1)}, u32[]{:S(2)}, u32[]{:S(2)}) collective-permute-start(bf16[516,576]{1,0:T(8,128)(2,1)S(1)} %pad_maximum_fusion.1), channel_id=1, source_target_pairs={{0,256},{1,257},{2,258},{3,259},{4,260},{5,261},{6,262},{7,263},{8... | collective-permute-start | bytes 1783304 | tf_op jit(solution)/shard_map/ppermute | solution.py:16
  27.2 15.6 %collective-permute-start.1 = (bf16[516,576]{1,0:T(8,128)(2,1)S(1)}, bf16[516,576]{1,0:T(8,128)(2,1)S(1)}, u32[]{:S(2)}, u32[]{:S(2)}) collective-permute-start(bf16[516,576]{1,0:T(8,128)(2,1)S(1)} %collective-permute-done), channel_id=1, source_target_pairs={{0,2},{2,0},{4,6},{6,4},{8,10},{10,8},{12,14},{14,12},{16,18},{18,... | collective-permute-start | bytes 1783304 | tf_op jit(solution)/shard_map/ppermute | solution.py:20
  42.9 1.4 %copy-start.2 = (bf16[1,256,1024]{2,1,0:T(8,128)(2,1)S(1)}, bf16[1,256,1024]{2,1,0:T(8,128)(2,1)}, u32[]{:S(2)}) copy-start(bf16[1,256,1024]{2,1,0:T(8,128)(2,1)} %all_gather.6) | copy-start | bytes 1572868
  47.4 20.8 %copy-start.4 = (bf16[1,2,2,576]{3,2,1,0:T(2,128)(2,1)S(1)}, bf16[1,2,2,576]{3,2,1,0:T(2,128)(2,1)}, u32[]{:S(2)}) copy-start(bf16[1,2,2,576]{3,2,1,0:T(2,128)(2,1)} %param.14) | copy-start | bytes 13828
  47.4 22.1 %copy-start.5 = (s32[16,8]{0,1:T(8,128)S(1)}, s32[16,8]{0,1:T(8,128)}, u32[]{:S(2)}) copy-start(s32[16,8]{0,1:T(8,128)} %param.9) | copy-start | bytes 1540
  47.4 22.7 %copy-start.6 = (f32[16,8]{0,1:T(8,128)S(1)}, f32[16,8]{0,1:T(8,128)}, u32[]{:S(2)}) copy-start(f32[16,8]{0,1:T(8,128)} %param.10) | copy-start | bytes 1540
  47.5 23.4 %copy-start.7 = (s32[256]{0:T(256)S(1)}, s32[256]{0:T(256)}, u32[]{:S(2)}) copy-start(s32[256]{0:T(256)} %param.15) | copy-start | bytes 3076
  48.8 69.5 %all-to-all-start = ((bf16[1,128,2,1792]{3,2,0,1:T(2,128)(2,1)}), bf16[1,128,2,1792]{3,2,0,1:T(2,128)(2,1)S(1)}, u32[]{:S(2)}, u32[]{:S(2)}) async-start(bf16[1,128,2,1792]{3,2,0,1:T(2,128)(2,1)} %bitcast.2), calls=%async_computation | async-start | bytes 1835008 | tf_op jit(solution)/shard_map/all_to_all | solution.py:58
  97.3 3.9 %copy-start.1 = (bf16[2,1024,576]{2,1,0:T(8,128)(2,1)S(1)}, bf16[2,1024,576]{2,1,0:T(8,128)(2,1)}, u32[]{:S(2)}) copy-start(bf16[2,1024,576]{2,1,0:T(8,128)(2,1)} %all-gather.2.cloned.1.call-done) | copy-start | bytes 7077892
Sparse Core Ops, SparseCore 0:
  44.4 52.9 all-gather.1
where the time goes:
time: 128 us; the launch traced here: 127 us
  waiting for transfers between devices  54.8 us (43%)
  starting transfers between devices  24.2 us (19%)
  between operations  18.2 us (14%)
  blocking collectives  10.2 us (8%)
  matrix products  8.8 us (7%)
  local copies, waits for them, and re-layouts  7.01 us (5%)
  other arithmetic  4.21 us (3%)
    all_gather x1, waiting for transfers between devices, local(): shard_rows = lax.all_gather(group_caches, 'tp', axis=1, tiled=True)  23.2 us
    all_to_all x1, starting transfers between devices, local(): lax.all_to_all(sent_rows, 'ep', split_axis=1, concat_axis=0, tiled=True)  19.4 us
    ppermute x1, waiting for transfers between devices, passed_along(): return lax.ppermute(value, axis, pairs)  16.4 us
    all_to_all x1, waiting for transfers between devices, local(): lax.all_to_all(sent_rows, 'ep', split_axis=1, concat_axis=0, tiled=True)  15.2 us
    all_gather x1, blocking collectives, local(): lax.all_gather(expert_hidden, 'tp', axis=2, tiled=True)  10.2 us
    ppermute x1, starting transfers between devices, swapped(): lax.ppermute(value, axis, [(i, i ^ 1 << apart) for i in range(lax.axis_si...  3.44 us
    dot_general x1, matrix products, local(): jnp.einsum('erh,ehd->erd', lax.all_gather(expert_hidden, 'tp', axis=2, ti...  3.16 us
    dot_general x1, matrix products, local(): jnp.einsum('gshl,gpl->gshp', query_set, shard_rows, preferred_element_typ...  2.93 us
  transfers between devices with their start and end apart: 4, of which 3 were waited for; matrix products, arithmetic and copies ran while one was open for 11% of the time, Pallas kernels for 0%

commit v1 on v0

v1 whole, which is shorter than its diff:
```python
import functools
import types

import jax
import jax.numpy as jnp
from jax import lax
from jax.experimental import pallas as pl
from jax.experimental.pallas import tpu as pltpu
from jax.sharding import PartitionSpec as P

MESH = pl.DeviceIdType.MESH
F32 = jnp.float32
BF16 = jnp.bfloat16

SCORE_SCALE = 0.07216878364870322
VERY_LOW = -1e30
VLAT = 512
LAT = 576
SHARD = 512
PLANES = 16
LOW = 8
TOK = 16
WIDTH = 1792
HALF = 512
QROWS = 128
SPAN = 16
CHUNKS = (896, 896)

OFFSETS = (1, -3, 5, -7, 3, -1, 7, -5, -4, 4, 8, 2, -2, 6, -6, 0)
SENT = 11
FIRST_HOPS = ((0, 4, 1), (4, 4, -1), (8, 1, 2), (9, 2, -2))
SECOND_HOPS = (-2, 2, -6, 6)


def remote(src, dst, send, recv, device):
    return pltpu.make_async_remote_copy(
        src_ref=src, dst_ref=dst, send_sem=send, recv_sem=recv, device_id=device, device_id_type=MESH
    )


def wait_for(ref, sem):
    pltpu.make_async_copy(ref, ref, sem).wait()


def iota(shape, dim):
    return lax.broadcasted_iota(jnp.int32, shape, dim)


def dot(a, b, b_dim=0):
    return lax.dot_general(a, b, (((1,), (b_dim,)), ((), ())), preferred_element_type=F32)


def split(value):
    high = value.astype(BF16)
    return high, (value - high.astype(F32)).astype(BF16)


def offset_of(block):
    value = jnp.zeros_like(block)
    for number, offset in enumerate(OFFSETS):
        value = jnp.where(block == number, offset, value)
    return value


def signed_gates(routes, gates):
    names = iota((TOK, 128), 1)
    picked = jnp.zeros((TOK, 128), F32)
    weight = jnp.zeros((TOK, 128), F32)
    for pick in range(routes.shape[1]):
        here = routes[:, pick : pick + 1] == names
        picked = jnp.where(here, 1.0, picked)
        weight = jnp.where(here, gates[:, pick : pick + 1], weight)
    earlier = jnp.where(iota((TOK, TOK), 1) < iota((TOK, TOK), 0), 1.0, 0.0).astype(BF16)
    slot = dot(earlier, picked.astype(BF16))
    return jnp.where(slot > 0.5, -weight, weight)


def scores_of(query, keys, span, length, tp, extra_ok):
    visible = []
    scores = []
    for number, key in enumerate(keys):
        first = (tp if number == 0 else 1 - tp) * SHARD
        ok = iota((1, SHARD), 1) + first < length
        visible.append(ok)
        scores.append(jnp.where(ok, dot(query, key[...]) * SCORE_SCALE, VERY_LOW))
    scores.append(jnp.where(extra_ok, dot(query, span[...], 1) * SCORE_SCALE, VERY_LOW))
    visible.append(extra_ok)
    top = functools.reduce(jnp.maximum, [jnp.max(s, axis=1, keepdims=True) for s in scores])
    parts = [jnp.where(ok, jnp.exp(s - top), 0.0) for s, ok in zip(scores, visible)]
    total = sum(jnp.sum(part, axis=1, keepdims=True) for part in parts)
    value = dot(parts[-1].astype(BF16), span[:, :VLAT])
    for part, key in zip(parts, keys):
        value = value + dot(part.astype(BF16), key[:VLAT, :], 1)
    return top, total, value


def kernel(
    routes_hbm,
    gates_hbm,
    hidden_hbm,
    down_hbm,
    queries_hbm,
    span_hbm,
    lengths_hbm,
    destinations_hbm,
    cache_hbm,
    moe_ref,
    attention_ref,
    *scratch,
):
    ref = named(scratch)
    count = len(CHUNKS)
    starts = [sum(CHUNKS[:c]) for c in range(count)]

    role, ep, tp = lax.axis_index("role"), lax.axis_index("ep"), lax.axis_index("tp")
    z, low = ep // LOW, ep % LOW

    def along_z(step):
        return {"ep": lax.rem(z + step + PLANES, PLANES) * LOW + low}

    def in_plane(step):
        return {"ep": z * LOW + lax.rem(low + step, LOW)}

    partner = {"tp": 1 - tp}
    other_role = {"role": 1 - role}
    sibling = {"ep": z * LOW + low + 1 - 2 * (low % 2)}

    barrier = pltpu.get_barrier_semaphore()

    def greet(device):
        pl.semaphore_signal(barrier, inc=1, device_id=device, device_id_type=MESH)

    greet(partner)
    greet(other_role)

    @pl.loop(1, LOW)
    def _(step):
        greet(in_plane(step))

    @pl.loop(1, PLANES)
    def _(step):
        greet(along_z(step))

    local = ref.local_sem

    def fetch(number, source, target):
        copy = pltpu.make_async_copy(source, target, local.at[number])
        copy.start()
        return copy

    routes_here = fetch(0, routes_hbm, ref.routes)
    gates_here = fetch(1, gates_hbm, ref.gates)
    hidden_here = fetch(2, hidden_hbm, ref.hidden)
    down_here = fetch(3, down_hbm, ref.down)
    cache_here = fetch(4, cache_hbm, ref.cache)
    queries_here = fetch(5, queries_hbm, ref.queries)
    span_here = fetch(6, span_hbm, ref.span)
    lengths_here = fetch(7, lengths_hbm, ref.lengths)
    destinations_here = fetch(8, destinations_hbm, ref.destinations)

    pl.semaphore_wait(barrier, 2 + LOW - 1 + PLANES - 1)

    hidden_copy = remote(hidden_hbm, ref.hidden_in, ref.tp_sem.at[0], ref.tp_sem.at[1], partner)
    hidden_copy.start()
    swap_copy = remote(
        queries_hbm.at[pl.ds(QROWS, QROWS)], ref.query_swap, ref.swap_sem.at[0], ref.swap_sem.at[1], sibling
    )

    @pl.when(role == 1)
    def _():
        swap_copy.start()

    routes_here.wait()
    gates_here.wait()
    own_gates = signed_gates(ref.routes[...], ref.gates[...])
    ref.gates_out[...] = own_gates
    for number, offset in enumerate(OFFSETS):
        rows = pl.ds(number * TOK, TOK)
        if offset == 0:
            ref.gates_in[rows, :] = own_gates
        else:
            remote(
                ref.gates_out, ref.gates_in.at[rows], ref.gate_sem.at[0], ref.gate_sem.at[1], along_z(offset)
            ).start()

    index = iota((256, 1), 0)
    block = (index >> 1) & 15
    raw = (((z - offset_of(block)) & 15) << 4) + (((low + (index >> 5)) & 7) << 1) + (index & 1)
    order = jnp.where(iota((256, 256), 1) == raw, 1.0, 0.0).astype(BF16)
    ref.order[...] = order
    hidden_here.wait()
    ref.hidden_own[...] = dot(order, ref.hidden[...]).astype(BF16)
    down_here.wait()
    own_units = pl.ds(pl.multiple_of(tp * HALF, HALF), HALF)
    other_units = pl.ds(pl.multiple_of((1 - tp) * HALF, HALF), HALF)
    for c in range(count):
        columns = slice(starts[c], starts[c] + CHUNKS[c])
        ref.first_half[:, columns] = dot(ref.hidden_own[...], ref.down[own_units, columns])

    hidden_copy.wait_recv()
    ref.hidden_own[...] = dot(ref.order[...], ref.hidden_in[...]).astype(BF16)
    x_sem = ref.x_sem
    for c in range(count):
        columns = slice(starts[c], starts[c] + CHUNKS[c])
        rows_out = ref.first_half[:, columns] + dot(ref.hidden_own[...], ref.down[other_units, columns])
        rows_out = rows_out.astype(BF16)
        ref.x_in[c][0:32, :] = rows_out[0:32]
        ref.x_out[c][...] = rows_out[32:]

        @pl.loop(1, LOW)
        def _(step, c=c):
            rows = pl.ds(pl.multiple_of(step * 32 - 32, 32), 32)
            rows_in = pl.ds(pl.multiple_of(step * 32, 32), 32)
            remote(
                ref.x_out[c].at[rows], ref.x_in[c].at[rows_in], x_sem.at[0, c], x_sem.at[1, c], in_plane(step)
            ).start()

    cache_here.wait()
    cache_copy = remote(ref.cache, ref.cache_in, ref.tp_sem.at[2], ref.tp_sem.at[3], partner)
    cache_copy.start()
    queries_here.wait()
    span_here.wait()
    lengths_here.wait()
    destinations_here.wait()
    length = ref.lengths[role * 128 + ep]
    flipped = jnp.broadcast_to(ref.destinations[ep], (QROWS, 1)) != ep
    ask_copy = remote(ref.query_out, ref.query_in, ref.role_sem.at[0], ref.role_sem.at[1], other_role)

    @pl.when(role == 1)
    def _():
        swap_copy.wait_recv()
        swapped = ref.query_swap[...].astype(F32)
        ref.query_out[...] = jnp.where(flipped, swapped, ref.queries[QROWS:, :].astype(F32)).astype(BF16)
        ask_copy.start()

    wait_for(ref.gates_in.at[pl.ds(0, 15 * TOK)], ref.gate_sem.at[1])
    gates_in = ref.gates_in[...]
    column = iota((128, 256), 1)
    expert = z * LOW + ((low - (column >> 5)) & 7)
    mine = iota((128, 256), 0) == expert
    pick_first = jnp.where(mine & ((column & 1) == 0), 1.0, 0.0).astype(BF16)
    pick_second = jnp.where(mine & ((column & 1) == 1), 1.0, 0.0).astype(BF16)
    first_high, first_low = split(jnp.maximum(gates_in, 0.0))
    second_high, second_low = split(jnp.maximum(-gates_in, 0.0))
    same_block = ((iota((256, 256), 1) >> 1) & 15) == (iota((256, 256), 0) >> 4)
    gates_high = jnp.where(same_block, dot(first_high, pick_first) + dot(second_high, pick_second), 0.0)
    gates_low = jnp.where(same_block, dot(first_low, pick_first) + dot(second_low, pick_second), 0.0)
    ref.gates_high[...] = gates_high.astype(BF16)
    ref.gates_low[...] = gates_low.astype(BF16)

    def combine(c):
        wait_for(ref.x_in[c].at[pl.ds(32, 224)], x_sem.at[1, c])
        rows_in = ref.x_in[c][...]
        sums = dot(ref.gates_high[...], rows_in) + dot(ref.gates_low[...], rows_in)
        ref.first_out[c][...] = sums[: SENT * TOK].astype(BF16)
        ref.kept[c][...] = sums[SENT * TOK :]
        for first, blocks, step in FIRST_HOPS:
            rows = pl.ds(first * TOK, blocks * TOK)
            remote(
                ref.first_out[c].at[rows], ref.first_in[c].at[rows], x_sem.at[2, c], x_sem.at[3, c], along_z(step)
            ).start()

    def collect(c):
        wait_for(ref.first_in[c], x_sem.at[3, c])
        got = ref.first_in[c][...].astype(F32)
        sums = ref.kept[c][0:64, :] + got[0:64] + got[64:128]
        ref.second_out[c][0:16, :] = (sums[0:16] + got[144:160]).astype(BF16)
        ref.second_out[c][16:32, :] = (sums[16:32] + got[128:144]).astype(BF16)
        ref.second_out[c][32:48, :] = (sums[32:48] + got[160:176]).astype(BF16)
        ref.second_out[c][48:64, :] = sums[48:64].astype(BF16)
        for number, step in enumerate(SECOND_HOPS):
            rows = pl.ds(number * TOK, TOK)
            remote(
                ref.second_out[c].at[rows], ref.second_in[c].at[rows], x_sem.at[4, c], x_sem.at[5, c], along_z(step)
            ).start()

    def finish(c):
        wait_for(ref.second_in[c], x_sem.at[5, c])
        got = ref.second_in[c][...].astype(F32)
        total = ref.kept[c][64:80, :] + (got[0:16] + got[16:32]) + (got[32:48] + got[48:64])
        moe_ref[:, starts[c] : starts[c] + CHUNKS[c]] = total.astype(BF16)

    keys = (ref.cache, ref.cache_in)
    step_of = iota((QROWS, SPAN), 0) >> 6
    key_of = iota((QROWS, SPAN), 1)
    answer_copy = remote(ref.answer_out, ref.answer_in, ref.role_sem.at[2], ref.role_sem.at[3], other_role)
    back_copy = remote(ref.answer_in, ref.answer_swap, ref.swap_sem.at[2], ref.swap_sem.at[3], sibling)

    def attend_first():
        cache_copy.wait_recv()

        @pl.when(role == 0)
        def _():
            ask_copy.wait_recv()
            top, total, value = scores_of(ref.query_in[...], keys, ref.span, length, tp, key_of < 4)
            ref.answer_out[:, :VLAT] = value.astype(BF16)
            lane = iota((QROWS, 128), 1)
            packed = jnp.zeros((QROWS, 128), F32)
            for number, figure in enumerate((top, total)):
                rest = figure
                for piece in range(3):
                    part = rest.astype(BF16).astype(F32)
                    rest = rest - part
                    packed = jnp.where(lane == number * 3 + piece, part, packed)
            ref.answer_out[:, VLAT:] = packed.astype(BF16)
            answer_copy.start()

    def attend_own():
        _, total, value = scores_of(ref.queries[:QROWS, :], keys, ref.span, length, tp, key_of <= step_of)
        attention_ref[:QROWS, :] = (value / total).astype(BF16)

        @pl.when(role == 0)
        def _():
            _, total, value = scores_of(ref.queries[QROWS:, :], keys, ref.span, length, tp, key_of <= step_of + 2)
            attention_ref[QROWS:, :] = (value / total).astype(BF16)

    def attend_back():
        @pl.when(role == 1)
        def _():
            answer_copy.wait_recv()
            back_copy.start()

    def attend_last():
        @pl.when(role == 1)
        def _():
            own_ok = (key_of >= 2) & (key_of <= step_of + 2)
            top, total, value = scores_of(ref.queries[QROWS:, :], (), ref.span, length, tp, own_ok)
            back_copy.wait_recv()
            answer = jnp.where(flipped, ref.answer_swap[...].astype(F32), ref.answer_in[...].astype(F32))
            figures = answer[:, VLAT:]
            far_top = figures[:, 0:1] + figures[:, 1:2] + figures[:, 2:3]
            far_total = figures[:, 3:4] + figures[:, 4:5] + figures[:, 5:6]
            best = jnp.maximum(top, far_top)
            near, far = jnp.exp(top - best), jnp.exp(far_top - best)
            value = near * value + far * answer[:, :VLAT]
            attention_ref[QROWS:, :] = (value / (near * total + far * far_total)).astype(BF16)

    combine(0)
    combine(1)
    attend_first()
    collect(0)
    attend_own()
    collect(1)
    attend_back()
    finish(0)
    attend_last()
    finish(1)

    hidden_copy.wait_send()
    cache_copy.wait_send()
    wait_for(ref.gates_in.at[pl.ds(0, 15 * TOK)], ref.gate_sem.at[0])
    for c in range(count):
        wait_for(ref.x_out[c], x_sem.at[0, c])
        wait_for(ref.first_out[c], x_sem.at[2, c])
        wait_for(ref.second_out[c], x_sem.at[4, c])

    @pl.when(role == 0)
    def _():
        answer_copy.wait_send()

    @pl.when(role == 1)
    def _():
        swap_copy.wait_send()
        ask_copy.wait_send()
        back_copy.wait_send()


def scratch_table():
    dma = pltpu.SemaphoreType.DMA

    def each(rows, kind=BF16):
        return [pltpu.VMEM((rows, width), kind) for width in CHUNKS]

    return dict(
        routes=pltpu.VMEM((TOK, 8), jnp.int32),
        gates=pltpu.VMEM((TOK, 8), F32),
        hidden=pltpu.VMEM((256, HALF), BF16),
        hidden_in=pltpu.VMEM((256, HALF), BF16),
        hidden_own=pltpu.VMEM((256, HALF), BF16),
        order=pltpu.VMEM((256, 256), BF16),
        down=pltpu.VMEM((2 * HALF, WIDTH), BF16),
        first_half=pltpu.VMEM((256, WIDTH), F32),
        cache=pltpu.VMEM((LAT, SHARD), BF16),
        cache_in=pltpu.VMEM((LAT, SHARD), BF16),
        queries=pltpu.VMEM((2 * QROWS, LAT), BF16),
        query_swap=pltpu.VMEM((QROWS, LAT), BF16),
        query_out=pltpu.VMEM((QROWS, LAT), BF16),
        query_in=pltpu.VMEM((QROWS, LAT), BF16),
        answer_out=pltpu.VMEM((QROWS, VLAT + 128), BF16),
        answer_in=pltpu.VMEM((QROWS, VLAT + 128), BF16),
        answer_swap=pltpu.VMEM((QROWS, VLAT + 128), BF16),
        span=pltpu.VMEM((SPAN, LAT), BF16),
        lengths=pltpu.SMEM((256,), jnp.int32),
        destinations=pltpu.SMEM((128,), jnp.int32),
        gates_out=pltpu.VMEM((TOK, 128), F32),
        gates_in=pltpu.VMEM((PLANES * TOK, 128), F32),
        gates_high=pltpu.VMEM((256, 256), BF16),
        gates_low=pltpu.VMEM((256, 256), BF16),
        x_out=each(224),
        x_in=each(256),
        first_out=each(SENT * TOK),
        first_in=each(SENT * TOK),
        kept=each(80, F32),
        second_out=each(64),
        second_in=each(64),
        local_sem=dma((9,)),
        tp_sem=dma((4,)),
        role_sem=dma((4,)),
        swap_sem=dma((4,)),
        gate_sem=dma((2,)),
        x_sem=dma((6, len(CHUNKS))),
    )


def named(refs):
    table = scratch_table()
    refs = jax.tree.unflatten(jax.tree.structure(table), refs)
    return types.SimpleNamespace(**refs)


def local(
    routes,
    gate_weights,
    expert_hidden,
    down_weight,
    queries,
    new_latents,
    lengths,
    destinations,
    latent_cache,
):
    span = jnp.pad(new_latents.reshape(4, LAT), ((0, SPAN - 4), (0, 0)))
    moe, attention = pl.pallas_call(
        kernel,
        out_shape=(
            jax.ShapeDtypeStruct((TOK, WIDTH), BF16),
            jax.ShapeDtypeStruct((2 * QROWS, VLAT), BF16),
        ),
        in_specs=[pl.BlockSpec(memory_space=pl.ANY)] * 9,
        out_specs=(pl.BlockSpec(memory_space=pltpu.VMEM),) * 2,
        scratch_shapes=jax.tree.leaves(scratch_table()),
        compiler_params=pltpu.CompilerParams(collective_id=0, has_side_effects=True, vmem_limit_bytes=40 * 2**20),
    )(
        routes,
        gate_weights,
        expert_hidden[0],
        down_weight[0],
        queries.reshape(2 * QROWS, LAT),
        span,
        lengths,
        destinations,
        jnp.swapaxes(latent_cache[0], 0, 1),
    )
    return moe, attention.reshape(1, 2, 2, QROWS // 2, VLAT)


def solution(mesh):
    placed = (
        P(("role", "ep"), None),
        P(("role", "ep"), None),
        P(("role", "ep"), None, "tp"),
        P("ep", None, "tp"),
        P(("role", "ep"), None, None, "tp", None),
        P(("role", "ep"), None, None, None),
        P(),
        P(),
        P(("role", "ep"), "tp", None),
    )
    return jax.shard_map(
        local,
        mesh=mesh,
        in_specs=placed,
        out_specs=(P(("role", "ep"), "tp"), P(("role", "ep"), None, None, "tp", None)),
        check_vma=False,
    )
```

time: 128 us -> 68.6 us (0.54)
  the two profiles are of different devices: /device:TPU:57 before, /device:TPU:1 now
where the time goes in v1:
time: 68.6 us; the launch traced here: 68.3 us
  Pallas kernels  57.7 us (84%)
  local copies, waits for them, and re-layouts  9.91 us (14%)
    pallas_call x1, Pallas kernels, local(): pl.pallas_call(kernel, out_shape=(jax.ShapeDtypeStruct((TOK, WIDTH), BF16...  57.7 us
    unnamed x16, local copies, waits for them, and re-layouts  9.19 us

profile of v1, /device:TPU:1, one launch (start us, length us, event | category | flops | bytes accessed | tf_op | source)
XLA Modules:
  0.0 68.3 jit_solution(6060605928844153555)
XLA Ops:
  0.6 0.7 %reshape.14 = bf16[4,576]{1,0:T(4,128)(2,1)S(1)} reshape(bf16[1,2,2,576]{3,2,1,0:T(2,128)(2,1)} %param.14) | data formatting | bytes 9216 | tf_op jit(solution)/shard_map/reshape | solution.py:432
  1.3 0.8 %copy.11.routes_hbm = s32[16,8]{1,0:T(8,128)S(1)} copy(s32[16,8]{0,1:T(8,128)} %param.9) | data formatting | bytes 1024 | tf_op args[0]
  2.1 0.8 %copy.12.gates_hbm = f32[16,8]{1,0:T(8,128)S(1)} copy(f32[16,8]{0,1:T(8,128)} %param.10) | data formatting | bytes 1024 | tf_op args[1]
  2.9 0.0 copy-start
  2.9 2.0 %copy-done = bf16[1,1024,1792]{2,1,0:T(8,128)(2,1)S(1)} copy-done((bf16[1,1024,1792]{2,1,0:T(8,128)(2,1)S(1)}, bf16[1,1024,1792]{2,1,0:T(8,128)(2,1)}, u32[]{:S(2)}) %copy-start) | copy-done | bytes 3670040
  4.9 0.0 copy-start.1
  4.9 1.1 %copy-done.1 = bf16[1,512,576]{1,2,0:T(8,128)(2,1)S(1)} copy-done((bf16[1,512,576]{1,2,0:T(8,128)(2,1)S(1)}, bf16[1,512,576]{1,2,0:T(8,128)(2,1)}, u32[]{:S(2)}) %copy-start.1) | copy-done | bytes 589848
  6.0 0.0 copy-start.2
  6.0 1.0 %copy-done.2 = bf16[1,2,2,64,576]{4,3,2,1,0:T(8,128)(2,1)S(1)} copy-done((bf16[1,2,2,64,576]{4,3,2,1,0:T(8,128)(2,1)S(1)}, bf16[1,2,2,64,576]{4,3,2,1,0:T(8,128)(2,1)}, u32[]{:S(2)}) %copy-start.2) | copy-done | bytes 294936
  6.9 0.0 copy-start.3
  6.9 0.9 %copy-done.3 = bf16[1,256,512]{2,1,0:T(8,128)(2,1)S(1)} copy-done((bf16[1,256,512]{2,1,0:T(8,128)(2,1)S(1)}, bf16[1,256,512]{2,1,0:T(8,128)(2,1)}, u32[]{:S(2)}) %copy-start.3) | copy-done | bytes 262168
  7.9 0.0 copy-start.4
  7.9 0.7 copy-done.4
  8.6 0.0 copy-start.5
  8.6 0.7 copy-done.5
  9.2 57.7 %shard_map.104 = (bf16[16,1792]{1,0:T(8,128)(2,1)S(1)}, bf16[256,512]{1,0:T(8,128)(2,1)S(1)}) custom-call(s32[16,8]{1,0:T(8,128)S(1)} %copy.11.routes_hbm, f32[16,8]{1,0:T(8,128)S(1)} %copy.12.gates_hbm, bf16[256,512]{1,0:T(8,128)(2,1)S(1)} %bitcast.10, bf16[1024,1792]{1,0:T(8,128)(2,1)S(1)} %bitcast.7, bf16[256,576]{1,0:T(8,128)(2,1)S(1)} %bitcast.9, ...), custom_call_target="tpu_custom_call" | custom-call | tf_op jit(solution)/shard_map/pallas_call | solution.py:433
  66.9 0.6 copy.15
  67.6 0.7 %copy.16 = bf16[1,2,2,64,512]{4,3,2,1,0:T(8,128)(2,1)} copy(bf16[1,2,2,64,512]{4,3,2,1,0:T(8,128)(2,1)S(1)} %bitcast.11) | data formatting | bytes 524288
  (1 shorter events, 0.0 us)
Async XLA Ops:
  2.9 2.0 %copy-start = (bf16[1,1024,1792]{2,1,0:T(8,128)(2,1)S(1)}, bf16[1,1024,1792]{2,1,0:T(8,128)(2,1)}, u32[]{:S(2)}) copy-start(bf16[1,1024,1792]{2,1,0:T(8,128)(2,1)} %param.12) | copy-start | bytes 11010052
  4.9 1.1 %copy-start.1 = (bf16[1,512,576]{1,2,0:T(8,128)(2,1)S(1)}, bf16[1,512,576]{1,2,0:T(8,128)(2,1)}, u32[]{:S(2)}) copy-start(bf16[1,512,576]{1,2,0:T(8,128)(2,1)} %param.17) | copy-start | bytes 1769476
  6.0 1.0 %copy-start.2 = (bf16[1,2,2,64,576]{4,3,2,1,0:T(8,128)(2,1)S(1)}, bf16[1,2,2,64,576]{4,3,2,1,0:T(8,128)(2,1)}, u32[]{:S(2)}) copy-start(bf16[1,2,2,64,576]{4,3,2,1,0:T(8,128)(2,1)} %param.13) | copy-start | bytes 884740
  6.9 0.9 %copy-start.3 = (bf16[1,256,512]{2,1,0:T(8,128)(2,1)S(1)}, bf16[1,256,512]{2,1,0:T(8,128)(2,1)}, u32[]{:S(2)}) copy-start(bf16[1,256,512]{2,1,0:T(8,128)(2,1)} %param.11) | copy-start | bytes 786436
  7.9 0.7 copy-start.4
  8.6 0.7 copy-start.5

commit v2 on v1

v2 whole, which is shorter than its diff:
```python
import functools
import types

import jax
import jax.numpy as jnp
from jax import lax
from jax.experimental import pallas as pl
from jax.experimental.pallas import tpu as pltpu
from jax.sharding import PartitionSpec as P

MESH = pl.DeviceIdType.MESH
F32 = jnp.float32
BF16 = jnp.bfloat16

SCORE_SCALE = 0.07216878364870322
VERY_LOW = -1e30
VLAT = 512
LAT = 576
SHARD = 512
PLANES = 16
LOW = 8
TOK = 16
WIDTH = 1792
HALF = 512
QROWS = 128
SPAN = 16
PART = 128
EDGE = 896

FAR = (5, -7, 7, -5, 8, 6, -6, 0)
NEAR = (1, -3, 3, -1, 4, -4, 2, -2)
HALVES = (FAR, NEAR)


class Chunk:
    def __init__(self, half, column, columns, sent, first_hops, planes, teams, second_hops):
        self.half = half
        self.columns = pl.ds(column, columns)
        self.sent = sent
        self.first_hops = first_hops
        self.planes = planes
        self.teams = teams
        self.second_hops = second_hops


CHUNKS = (
    Chunk(0, 0, EDGE, 5, ((0, 2, 1), (2, 2, -1), (4, 1, -2)), (-1, -1, 1, 1, 2, 0, 0, 0), (0, 1, 0, 1, 0, 0, 1, 2), (-6, 6)),
    Chunk(0, EDGE, EDGE, 5, ((0, 2, 1), (2, 2, -1), (4, 1, 2)), (-1, -1, 1, 1, -2, 0, 0, 0), (0, 1, 0, 1, 1, 0, 1, 2), (-6, 6)),
    Chunk(
        1, 0, WIDTH, 6, ((0, 2, 1), (2, 2, -1), (4, 1, -2), (5, 1, 2)), (-1, -1, 1, 1, 2, -2, 0, 0), (0, 1, 0, 1, 0, 1, 0, 1), (-2, 2)
    ),
)


def remote(src, dst, send, recv, device):
    return pltpu.make_async_remote_copy(
        src_ref=src, dst_ref=dst, send_sem=send, recv_sem=recv, device_id=device, device_id_type=MESH
    )


def wait_for(ref, sem):
    pltpu.make_async_copy(ref, ref, sem).wait()


def iota(shape, dim):
    return lax.broadcasted_iota(jnp.int32, shape, dim)


def dot(a, b, b_dim=0):
    return lax.dot_general(a, b, (((1,), (b_dim,)), ((), ())), preferred_element_type=F32)


def split(value):
    high = value.astype(BF16)
    return high, (value - high.astype(F32)).astype(BF16)


def choose(index, values):
    result = jnp.zeros_like(index)
    for number, value in enumerate(values):
        result = jnp.where(index == number, value, result)
    return result


def signed_gates(routes, gates, spread):
    names = iota((128, TOK), 0)
    picked = jnp.zeros((128, TOK), F32)
    weight = jnp.zeros((128, TOK), F32)
    for pick in range(routes.shape[0]):
        here = routes[pick : pick + 1, :] == names
        picked = jnp.where(here, 1.0, picked)
        weight = jnp.where(here, gates[pick : pick + 1, :], weight)
    earlier = jnp.where(iota((TOK, TOK), 0) < iota((TOK, TOK), 1), 1.0, 0.0).astype(BF16)
    slot = dot(picked.astype(BF16), earlier)
    spread[...] = jnp.zeros_like(spread)
    spread[:, :TOK] = jnp.where(slot > 0.5, -weight, weight)
    return spread[...].T[:TOK, :]


def scores_of(query, keys, span, length, tp, extra_ok):
    visible = []
    scores = []
    for number, key in enumerate(keys):
        first = (tp if number == 0 else 1 - tp) * SHARD
        ok = iota((1, SHARD), 1) + first < length
        visible.append(ok)
        scores.append(jnp.where(ok, dot(query, key[...]) * SCORE_SCALE, VERY_LOW))
    scores.append(jnp.where(extra_ok, dot(query, span[...], 1) * SCORE_SCALE, VERY_LOW))
    visible.append(extra_ok)
    top = functools.reduce(jnp.maximum, [jnp.max(s, axis=1, keepdims=True) for s in scores])
    parts = [jnp.where(ok, jnp.exp(s - top), 0.0) for s, ok in zip(scores, visible)]
    total = sum(jnp.sum(part, axis=1, keepdims=True) for part in parts)
    value = dot(parts[-1].astype(BF16), span[:, :VLAT])
    for part, key in zip(parts, keys):
        value = value + dot(part.astype(BF16), key[:VLAT, :], 1)
    return top, total, value


def kernel(
    routes_hbm,
    gates_hbm,
    hidden_hbm,
    down_hbm,
    queries_hbm,
    span_hbm,
    lengths_hbm,
    destinations_hbm,
    cache_hbm,
    moe_ref,
    attention_ref,
    *scratch,
):
    ref = named(scratch)

    role, ep, tp = lax.axis_index("role"), lax.axis_index("ep"), lax.axis_index("tp")
    z, low = ep // LOW, ep % LOW

    def along_z(step):
        return {"ep": lax.rem(z + step + PLANES, PLANES) * LOW + low}

    def in_plane(step):
        return {"ep": z * LOW + lax.rem(low + step, LOW)}

    partner = {"tp": 1 - tp}
    other_role = {"role": 1 - role}
    sibling = {"ep": z * LOW + low + 1 - 2 * (low % 2)}

    barrier = pltpu.get_barrier_semaphore()

    def greet(device):
        pl.semaphore_signal(barrier, inc=1, device_id=device, device_id_type=MESH)

    greet(partner)
    greet(other_role)

    @pl.loop(1, LOW)
    def _(step):
        greet(in_plane(step))

    for step in (1, -1, 2, -2):
        greet(along_z(step))

    local = ref.local_sem

    def fetch(number, source, target):
        copy = pltpu.make_async_copy(source, target, local.at[number])
        copy.start()
        return copy

    routes_here = fetch(0, routes_hbm, ref.routes)
    gates_here = fetch(1, gates_hbm, ref.gates)
    down_here = fetch(3, down_hbm, ref.down)
    cache_here = fetch(4, cache_hbm, ref.cache)
    queries_here = fetch(5, queries_hbm, ref.queries)
    span_here = fetch(6, span_hbm, ref.latents)
    lengths_here = fetch(7, lengths_hbm, ref.lengths)
    destinations_here = fetch(8, destinations_hbm, ref.destinations)

    def plane_rows(offset):
        return pl.ds(pl.multiple_of(((z - offset) & 15) * TOK, TOK), TOK)

    for half, offsets in enumerate(HALVES):
        for number, offset in enumerate(offsets):
            pltpu.make_async_copy(
                hidden_hbm.at[plane_rows(offset)], ref.hidden.at[half, pl.ds(number * TOK, TOK)], local.at[2]
            ).start()

    routes_here.wait()
    gates_here.wait()
    ref.gates_out[...] = signed_gates(ref.routes[...], ref.gates[...], ref.spread)
    index = iota((PART, 1), 0)
    raw = (((index >> 1) & 7) << 4) + (((low + (index >> 4)) & 7) << 1) + (index & 1)
    ref.order[...] = jnp.where(iota((PART, PART), 1) == raw, 1.0, 0.0).astype(BF16)

    pl.semaphore_wait(barrier, 2 + LOW - 1 + 4)

    for half, offsets in enumerate(HALVES):
        for number, offset in enumerate(offsets):
            remote(
                hidden_hbm.at[plane_rows(offset)],
                ref.hidden_in.at[half, pl.ds(number * TOK, TOK)],
                ref.hidden_sem.at[0, half],
                ref.hidden_sem.at[1, half],
                partner,
            ).start()
    swap_copy = remote(
        queries_hbm.at[pl.ds(QROWS, QROWS)], ref.query_swap, ref.swap_sem.at[0], ref.swap_sem.at[1], sibling
    )

    @pl.when(role == 1)
    def _():
        swap_copy.start()

    def pass_gates(stage):
        for side, step in enumerate((2, -2)):
            source = ref.gates_out
            if stage > 0:
                source = ref.gates_in.at[stage - 1, side]
                wait_for(source, ref.gate_sem.at[1, stage - 1, side])
            if stage < 3:
                remote(
                    source,
                    ref.gates_in.at[stage, side],
                    ref.gate_sem.at[0, stage, side],
                    ref.gate_sem.at[1, stage, side],
                    along_z(step),
                ).start()

    pass_gates(0)

    own_units = pl.ds(pl.multiple_of(tp * HALF, HALF), HALF)
    other_units = pl.ds(pl.multiple_of((1 - tp) * HALF, HALF), HALF)
    wait_for(ref.hidden, local.at[2])
    down_here.wait()
    for half in range(2):
        ref.first_half[half] = dot(ref.hidden[half], ref.down[own_units, :])

    x_sem = ref.x_sem
    for c, chunk in enumerate(CHUNKS):
        half, columns, sent = chunk.half, chunk.columns, chunk.sent * TOK
        if columns.start == 0:
            wait_for(ref.hidden_in.at[half], ref.hidden_sem.at[1, half])
        rows = ref.first_half[half, :, columns] + dot(ref.hidden_in[half], ref.down[other_units, columns])
        rows = rows.astype(BF16)
        ref.first_out[half, 0:sent, columns] = rows[:sent]
        ref.first_in[half, sent:, columns] = rows[sent:]
        for first, blocks, step in chunk.first_hops:
            place = (half, pl.ds(first * TOK, blocks * TOK), columns)
            remote(ref.first_out.at[place], ref.first_in.at[place], x_sem.at[0, c], x_sem.at[1, c], along_z(step)).start()

    pass_gates(1)

    cache_here.wait()
    cache_copy = remote(ref.cache, ref.cache_in, ref.tp_sem.at[2], ref.tp_sem.at[3], partner)
    cache_copy.start()
    queries_here.wait()
    span_here.wait()
    latents = [ref.latents[group].astype(F32) for group in range(2)]
    ref.span[...] = jnp.concatenate(latents + [jnp.zeros((SPAN - 4, LAT), F32)], axis=0).astype(BF16)
    lengths_here.wait()
    destinations_here.wait()
    length = ref.lengths[role * 128 + ep]
    flipped = jnp.broadcast_to(ref.destinations[ep], (QROWS, 1)) != ep
    ask_copy = remote(ref.query_out, ref.query_in, ref.role_sem.at[0], ref.role_sem.at[1], other_role)

    @pl.when(role == 1)
    def _():
        swap_copy.wait_recv()
        swapped = ref.query_swap[...].astype(F32)
        ref.query_out[...] = jnp.where(flipped, swapped, ref.queries[QROWS:, :].astype(F32)).astype(BF16)
        ask_copy.start()

    pass_gates(2)

    def exchange(c):
        chunk = CHUNKS[c]
        half, columns = chunk.half, chunk.columns
        wait_for(ref.first_in.at[half, pl.ds(0, chunk.sent * TOK), columns], x_sem.at[1, c])
        rows = dot(ref.order[...], ref.first_in[half, :, columns]).astype(BF16)
        ref.x_in[half, 0:TOK, columns] = rows[0:TOK]
        ref.x_out[half, :, columns] = rows[TOK:]

        @pl.loop(1, LOW)
        def _(step):
            rows_out = pl.ds(pl.multiple_of(step * TOK - TOK, TOK), TOK)
            rows_in = pl.ds(pl.multiple_of(step * TOK, TOK), TOK)
            remote(
                ref.x_out.at[half, rows_out, columns],
                ref.x_in.at[half, rows_in, columns],
                x_sem.at[2, c],
                x_sem.at[3, c],
                in_plane(step),
            ).start()

    def gate_matrix(c):
        chunk = CHUNKS[c]
        sources = [ref.gates_in[2 if chunk.half == 0 else 0, side] for side in range(2)]
        if chunk.half == 0:
            sources.append(ref.gates_out[...])
        gates = jnp.concatenate(sources, axis=0)
        column = iota((128, PART), 1)
        plane = z + choose((iota((1, PART), 1) >> 1) & 7, chunk.planes)
        mine = iota((128, PART), 0) == (((plane & 15) << 3) + ((low - (column >> 4)) & 7))
        pick_first = jnp.where(mine & ((column & 1) == 0), 1.0, 0.0).astype(BF16)
        pick_second = jnp.where(mine & ((column & 1) == 1), 1.0, 0.0).astype(BF16)
        team = choose((iota((1, PART), 1) >> 1) & 7, chunk.teams)
        same_team = (iota((gates.shape[0], PART), 0) >> 4) == team
        first_high, first_low = split(jnp.maximum(gates, 0.0))
        second_high, second_low = split(jnp.maximum(-gates, 0.0))
        gates_high = jnp.where(same_team, dot(first_high, pick_first) + dot(second_high, pick_second), 0.0)
        gates_low = jnp.where(same_team, dot(first_low, pick_first) + dot(second_low, pick_second), 0.0)
        ref.gates_high[c, 0 : gates.shape[0], :] = gates_high.astype(BF16)
        ref.gates_low[c, 0 : gates.shape[0], :] = gates_low.astype(BF16)

    def combine(c):
        chunk = CHUNKS[c]
        half, columns = chunk.half, chunk.columns
        teams = 48 if half == 0 else 32
        wait_for(ref.x_in.at[half, pl.ds(TOK, PART - TOK), columns], x_sem.at[3, c])
        rows = ref.x_in[half, :, columns]
        sums = dot(ref.gates_high[c, 0:teams, :], rows) + dot(ref.gates_low[c, 0:teams, :], rows)
        ref.second_out[half, :, columns] = sums[:32].astype(BF16)
        if half == 0:
            ref.kept[:, columns] = sums[32:]
        for number, step in enumerate(chunk.second_hops):
            place = (half, pl.ds(number * TOK, TOK), columns)
            remote(ref.second_out.at[place], ref.second_in.at[place], x_sem.at[4, c], x_sem.at[5, c], along_z(step)).start()

    def finish():
        for c, chunk in enumerate(CHUNKS):
            wait_for(ref.second_in.at[chunk.half, :, chunk.columns], x_sem.at[5, c])
        total = ref.kept[...]
        for half in range(2):
            got = ref.second_in[half].astype(F32)
            total = total + (got[0:16] + got[16:32])
        moe_ref[...] = total.astype(BF16)

    keys = (ref.cache, ref.cache_in)
    step_of = iota((QROWS, SPAN), 0) >> 6
    key_of = iota((QROWS, SPAN), 1)
    answer_copy = remote(ref.answer_out, ref.answer_in, ref.role_sem.at[2], ref.role_sem.at[3], other_role)
    back_copy = remote(ref.answer_in, ref.answer_swap, ref.swap_sem.at[2], ref.swap_sem.at[3], sibling)

    def attend_first():
        cache_copy.wait_recv()

        @pl.when(role == 0)
        def _():
            ask_copy.wait_recv()
            top, total, value = scores_of(ref.query_in[...], keys, ref.span, length, tp, key_of < 4)
            ref.answer_out[:, :VLAT] = value.astype(BF16)
            lane = iota((QROWS, 128), 1)
            packed = jnp.zeros((QROWS, 128), F32)
            for number, figure in enumerate((top, total)):
                rest = figure
                for piece in range(3):
                    part = rest.astype(BF16).astype(F32)
                    rest = rest - part
                    packed = jnp.where(lane == number * 3 + piece, part, packed)
            ref.answer_out[:, VLAT:] = packed.astype(BF16)
            answer_copy.start()

    def attend_own():
        _, total, value = scores_of(ref.queries[:QROWS, :], keys, ref.span, length, tp, key_of <= step_of)
        attention_ref[:QROWS, :] = (value / total).astype(BF16)

        @pl.when(role == 0)
        def _():
            _, total, value = scores_of(ref.queries[QROWS:, :], keys, ref.span, length, tp, key_of <= step_of + 2)
            attention_ref[QROWS:, :] = (value / total).astype(BF16)

    def attend_back():
        @pl.when(role == 1)
        def _():
            answer_copy.wait_recv()
            back_copy.start()

    def attend_last():
        @pl.when(role == 1)
        def _():
            own_ok = (key_of >= 2) & (key_of <= step_of + 2)
            top, total, value = scores_of(ref.queries[QROWS:, :], (), ref.span, length, tp, own_ok)
            back_copy.wait_recv()
            answer = jnp.where(flipped, ref.answer_swap[...].astype(F32), ref.answer_in[...].astype(F32))
            figures = answer[:, VLAT:]
            far_top = figures[:, 0:1] + figures[:, 1:2] + figures[:, 2:3]
            far_total = figures[:, 3:4] + figures[:, 4:5] + figures[:, 5:6]
            best = jnp.maximum(top, far_top)
            near, far = jnp.exp(top - best), jnp.exp(far_top - best)
            value = near * value + far * answer[:, :VLAT]
            attention_ref[QROWS:, :] = (value / (near * total + far * far_total)).astype(BF16)

    exchange(0)
    exchange(1)
    pass_gates(3)
    for c in range(3):
        gate_matrix(c)
    exchange(2)
    combine(0)
    combine(1)
    combine(2)
    attend_first()
    attend_own()
    attend_back()
    attend_last()
    finish()

    cache_copy.wait_send()
    for stage in range(3):
        for side in range(2):
            wait_for(ref.gates_out, ref.gate_sem.at[0, stage, side])
    for half in range(2):
        wait_for(ref.hidden_in.at[half], ref.hidden_sem.at[0, half])
    for c, chunk in enumerate(CHUNKS):
        half, columns = chunk.half, chunk.columns
        wait_for(ref.first_out.at[half, pl.ds(0, chunk.sent * TOK), columns], x_sem.at[0, c])
        wait_for(ref.x_out.at[half, :, columns], x_sem.at[2, c])
        wait_for(ref.second_out.at[half, :, columns], x_sem.at[4, c])

    @pl.when(role == 0)
    def _():
        answer_copy.wait_send()

    @pl.when(role == 1)
    def _():
        swap_copy.wait_send()
        ask_copy.wait_send()
        back_copy.wait_send()


def scratch_table():
    dma = pltpu.SemaphoreType.DMA

    def each(rows, kind=BF16):
        return pltpu.VMEM((2, rows, WIDTH), kind)

    return dict(
        routes=pltpu.VMEM((8, TOK), jnp.int32),
        gates=pltpu.VMEM((8, TOK), F32),
        spread=pltpu.VMEM((128, 128), F32),
        hidden=pltpu.VMEM((2, PART, HALF), BF16),
        hidden_in=pltpu.VMEM((2, PART, HALF), BF16),
        order=pltpu.VMEM((PART, PART), BF16),
        down=pltpu.VMEM((2 * HALF, WIDTH), BF16),
        first_half=each(PART, F32),
        cache=pltpu.VMEM((LAT, SHARD), BF16),
        cache_in=pltpu.VMEM((LAT, SHARD), BF16),
        queries=pltpu.VMEM((2 * QROWS, LAT), BF16),
        query_swap=pltpu.VMEM((QROWS, LAT), BF16),
        query_out=pltpu.VMEM((QROWS, LAT), BF16),
        query_in=pltpu.VMEM((QROWS, LAT), BF16),
        answer_out=pltpu.VMEM((QROWS, VLAT + 128), BF16),
        answer_in=pltpu.VMEM((QROWS, VLAT + 128), BF16),
        answer_swap=pltpu.VMEM((QROWS, VLAT + 128), BF16),
        latents=pltpu.VMEM((2, 2, LAT), BF16),
        span=pltpu.VMEM((SPAN, LAT), BF16),
        lengths=pltpu.SMEM((256,), jnp.int32),
        destinations=pltpu.SMEM((128,), jnp.int32),
        gates_out=pltpu.VMEM((TOK, 128), F32),
        gates_in=pltpu.VMEM((3, 2, TOK, 128), F32),
        gates_high=pltpu.VMEM((3, 48, PART), BF16),
        gates_low=pltpu.VMEM((3, 48, PART), BF16),
        x_out=each(PART - TOK),
        x_in=each(PART),
        first_out=each(96),
        first_in=each(PART),
        kept=pltpu.VMEM((TOK, WIDTH), F32),
        second_out=each(32),
        second_in=each(32),
        local_sem=dma((9,)),
        tp_sem=dma((4,)),
        role_sem=dma((4,)),
        swap_sem=dma((4,)),
        gate_sem=dma((2, 3, 2)),
        x_sem=dma((6, 3)),
        hidden_sem=dma((2, 2)),
    )


def named(refs):
    table = scratch_table()
    refs = jax.tree.unflatten(jax.tree.structure(table), refs)
    return types.SimpleNamespace(**refs)


def local(
    routes,
    gate_weights,
    expert_hidden,
    down_weight,
    queries,
    new_latents,
    lengths,
    destinations,
    latent_cache,
):
    moe, attention = pl.pallas_call(
        kernel,
        out_shape=(
            jax.ShapeDtypeStruct((TOK, WIDTH), BF16),
            jax.ShapeDtypeStruct((2 * QROWS, VLAT), BF16),
        ),
        in_specs=[pl.BlockSpec(memory_space=pl.ANY)] * 9,
        out_specs=(pl.BlockSpec(memory_space=pltpu.VMEM),) * 2,
        scratch_shapes=jax.tree.leaves(scratch_table()),
        compiler_params=pltpu.CompilerParams(collective_id=0, has_side_effects=True, vmem_limit_bytes=63 * 2**20),
    )(
        routes.T,
        gate_weights.T,
        expert_hidden[0],
        down_weight[0],
        queries.reshape(2 * QROWS, LAT),
        new_latents[0],
        lengths,
        destinations,
        jnp.swapaxes(latent_cache[0], 0, 1),
    )
    return moe, attention.reshape(1, 2, 2, QROWS // 2, VLAT)


def solution(mesh):
    placed = (
        P(("role", "ep"), None),
        P(("role", "ep"), None),
        P(("role", "ep"), None, "tp"),
        P("ep", None, "tp"),
        P(("role", "ep"), None, None, "tp", None),
        P(("role", "ep"), None, None, None),
        P(),
        P(),
        P(("role", "ep"), "tp", None),
    )
    return jax.shard_map(
        local,
        mesh=mesh,
        in_specs=placed,
        out_specs=(P(("role", "ep"), "tp"), P(("role", "ep"), None, None, "tp", None)),
        check_vma=False,
    )
```

time: 68.6 us -> 55.8 us (0.81)
  local copies, waits for them, and re-layouts: 9.91 us -> 3.11 us
  Pallas kernels: 57.7 us -> 51.8 us
    unnamed x16 -> x2, local copies, waits for them, and re-layouts: 9.19 us -> 3.11 us
    pallas_call x1, Pallas kernels: 57.7 us -> 51.8 us  [local(): pl.pallas_call(kernel, out_shape=(jax.ShapeDtypeStruct((TOK, WIDTH), BF16...]
    reshape x1 -> x0, local copies, waits for them, and re-layouts: 0.71 us -> none  [local(): span = jnp.pad(new_latents.reshape(4, LAT), ((0, SPAN - 4), (0, 0)))]
where the time goes in v2:
time: 55.8 us; the launch traced here: 55.6 us
  Pallas kernels  51.8 us (93%)
  local copies, waits for them, and re-layouts  3.11 us (6%)
  between operations  0.64 us (1%)
    pallas_call x1, Pallas kernels, local(): pl.pallas_call(kernel, out_shape=(jax.ShapeDtypeStruct((TOK, WIDTH), BF16...  51.8 us
    unnamed x2, local copies, waits for them, and re-layouts  3.11 us

profile of v2, /device:TPU:1, one launch (start us, length us, event | category | flops | bytes accessed | tf_op | source)
XLA Modules:
  0.0 55.6 jit_solution(9548884530963151138)
XLA Ops:
  0.6 51.8 %shard_map.104 = (bf16[16,1792]{1,0:T(8,128)(2,1)}, bf16[256,512]{1,0:T(8,128)(2,1)}) custom-call(s32[8,16]{1,0:T(8,128)} %bitcast.16, f32[8,16]{1,0:T(8,128)} %bitcast.17, bf16[256,512]{1,0:T(8,128)(2,1)} %bitcast.14, bf16[1024,1792]{1,0:T(8,128)(2,1)} %bitcast.10, bf16[256,576]{1,0:T(8,128)(2,1)} %bitcast.12, bf16[2,2,576]{2,1,0:T(2,128)(2,1)} %bitcast.15, ...), custom_call_target="tpu_custom_call" | custom-call | tf_op jit(solution)/shard_map/pallas_call | solution.py:497
  52.5 1.4 %copy.13 = bf16[16,1792]{1,0:T(8,128)(2,1)} copy(bf16[16,1792]{1,0:T(8,128)(2,1)} %get-tuple-element.8) | data formatting | bytes 114688
  53.9 1.7 %copy.14 = bf16[1,2,2,64,512]{4,3,2,1,0:T(8,128)(2,1)} copy(bf16[1,2,2,64,512]{4,3,2,1,0:T(8,128)(2,1)} %bitcast.13) | data formatting | bytes 524288

commit v3 on v2

--- a/solution.py
+++ b/solution.py
@@ -33,23 +33,28 @@
 
 
 class Chunk:
-    def __init__(self, half, column, columns, sent, first_hops, planes, teams, second_hops):
+    def __init__(self, half, column, columns):
         self.half = half
+        self.kind = 2 if half == 1 else int(column >= EDGE)
         self.columns = pl.ds(column, columns)
-        self.sent = sent
-        self.first_hops = first_hops
-        self.planes = planes
-        self.teams = teams
-        self.second_hops = second_hops
-
-
-CHUNKS = (
-    Chunk(0, 0, EDGE, 5, ((0, 2, 1), (2, 2, -1), (4, 1, -2)), (-1, -1, 1, 1, 2, 0, 0, 0), (0, 1, 0, 1, 0, 0, 1, 2), (-6, 6)),
-    Chunk(0, EDGE, EDGE, 5, ((0, 2, 1), (2, 2, -1), (4, 1, 2)), (-1, -1, 1, 1, -2, 0, 0, 0), (0, 1, 0, 1, 1, 0, 1, 2), (-6, 6)),
-    Chunk(
-        1, 0, WIDTH, 6, ((0, 2, 1), (2, 2, -1), (4, 1, -2), (5, 1, 2)), (-1, -1, 1, 1, 2, -2, 0, 0), (0, 1, 0, 1, 0, 1, 0, 1), (-2, 2)
-    ),
-)
+        near = half == 1
+        left = column < EDGE
+        self.sent = 6 if near else 5
+        if near:
+            far_hops = ((4, 1, -2), (5, 1, 2))
+        else:
+            far_hops = ((4, 1, -2 if left else 2),)
+        self.first_hops = ((0, 2, 1), (2, 2, -1)) + far_hops
+        if near:
+            self.planes = (-1, -1, 1, 1, 2, -2, 0, 0)
+            self.teams = (0, 1, 0, 1, 0, 1, 0, 1)
+        else:
+            self.planes = (-1, -1, 1, 1, 2 if left else -2, 0, 0, 0)
+            self.teams = (0, 1, 0, 1, 0 if left else 1, 0, 1, 2)
+        self.second_hops = (-2, 2) if near else (-6, 6)
+
+
+CHUNKS = tuple(Chunk(*each) for each in ((0, 0, 896), (0, 896, 896), (1, 0, 896), (1, 896, 896)))
 
 
 def remote(src, dst, send, recv, device):
@@ -234,11 +239,14 @@
     down_here.wait()
     for half in range(2):
         ref.first_half[half] = dot(ref.hidden[half], ref.down[own_units, :])
+    pass_gates(1)
 
     x_sem = ref.x_sem
     for c, chunk in enumerate(CHUNKS):
         half, columns, sent = chunk.half, chunk.columns, chunk.sent * TOK
         if columns.start == 0:
+            if half == 1:
+                pass_gates(2)
             wait_for(ref.hidden_in.at[half], ref.hidden_sem.at[1, half])
         rows = ref.first_half[half, :, columns] + dot(ref.hidden_in[half], ref.down[other_units, columns])
         rows = rows.astype(BF16)
@@ -247,8 +255,6 @@
         for first, blocks, step in chunk.first_hops:
             place = (half, pl.ds(first * TOK, blocks * TOK), columns)
             remote(ref.first_out.at[place], ref.first_in.at[place], x_sem.at[0, c], x_sem.at[1, c], along_z(step)).start()
-
-    pass_gates(1)
 
     cache_here.wait()
     cache_copy = remote(ref.cache, ref.cache_in, ref.tp_sem.at[2], ref.tp_sem.at[3], partner)
@@ -270,8 +276,6 @@
         ref.query_out[...] = jnp.where(flipped, swapped, ref.queries[QROWS:, :].astype(F32)).astype(BF16)
         ask_copy.start()
 
-    pass_gates(2)
-
     def exchange(c):
         chunk = CHUNKS[c]
         half, columns = chunk.half, chunk.columns
@@ -292,8 +296,7 @@
                 in_plane(step),
             ).start()
 
-    def gate_matrix(c):
-        chunk = CHUNKS[c]
+    def gate_matrix(chunk):
         sources = [ref.gates_in[2 if chunk.half == 0 else 0, side] for side in range(2)]
         if chunk.half == 0:
             sources.append(ref.gates_out[...])
@@ -309,8 +312,8 @@
         second_high, second_low = split(jnp.maximum(-gates, 0.0))
         gates_high = jnp.where(same_team, dot(first_high, pick_first) + dot(second_high, pick_second), 0.0)
         gates_low = jnp.where(same_team, dot(first_low, pick_first) + dot(second_low, pick_second), 0.0)
-        ref.gates_high[c, 0 : gates.shape[0], :] = gates_high.astype(BF16)
-        ref.gates_low[c, 0 : gates.shape[0], :] = gates_low.astype(BF16)
+        ref.gates_high[chunk.kind, 0 : gates.shape[0], :] = gates_high.astype(BF16)
+        ref.gates_low[chunk.kind, 0 : gates.shape[0], :] = gates_low.astype(BF16)
 
     def combine(c):
         chunk = CHUNKS[c]
@@ -318,7 +321,7 @@
         teams = 48 if half == 0 else 32
         wait_for(ref.x_in.at[half, pl.ds(TOK, PART - TOK), columns], x_sem.at[3, c])
         rows = ref.x_in[half, :, columns]
-        sums = dot(ref.gates_high[c, 0:teams, :], rows) + dot(ref.gates_low[c, 0:teams, :], rows)
+        sums = dot(ref.gates_high[chunk.kind, 0:teams, :], rows) + dot(ref.gates_low[chunk.kind, 0:teams, :], rows)
         ref.second_out[half, :, columns] = sums[:32].astype(BF16)
         if half == 0:
             ref.kept[:, columns] = sums[32:]
@@ -393,12 +396,14 @@
     exchange(0)
     exchange(1)
     pass_gates(3)
-    for c in range(3):
-        gate_matrix(c)
+    for chunk in {chunk.kind: chunk for chunk in CHUNKS}.values():
+        gate_matrix(chunk)
     exchange(2)
     combine(0)
+    exchange(3)
     combine(1)
     combine(2)
+    combine(3)
     attend_first()
     attend_own()
     attend_back()
@@ -472,7 +477,7 @@
         role_sem=dma((4,)),
         swap_sem=dma((4,)),
         gate_sem=dma((2, 3, 2)),
-        x_sem=dma((6, 3)),
+        x_sem=dma((6, len(CHUNKS))),
         hidden_sem=dma((2, 2)),
     )
 
@@ -494,17 +499,7 @@
     destinations,
     latent_cache,
 ):
-    moe, attention = pl.pallas_call(
-        kernel,
-        out_shape=(
-            jax.ShapeDtypeStruct((TOK, WIDTH), BF16),
-            jax.ShapeDtypeStruct((2 * QROWS, VLAT), BF16),
-        ),
-        in_specs=[pl.BlockSpec(memory_space=pl.ANY)] * 9,
-        out_specs=(pl.BlockSpec(memory_space=pltpu.VMEM),) * 2,
-        scratch_shapes=jax.tree.leaves(scratch_table()),
-        compiler_params=pltpu.CompilerParams(collective_id=0, has_side_effects=True, vmem_limit_bytes=63 * 2**20),
-    )(
+    operands = (
         routes.T,
         gate_weights.T,
         expert_hidden[0],
@@ -515,6 +510,18 @@
         destinations,
         jnp.swapaxes(latent_cache[0], 0, 1),
     )
+    operands = [pltpu.with_memory_space_constraint(operand, pltpu.HBM) for operand in operands]
+    moe, attention = pl.pallas_call(
+        kernel,
+        out_shape=(
+            jax.ShapeDtypeStruct((TOK, WIDTH), BF16),
+            jax.ShapeDtypeStruct((2 * QROWS, VLAT), BF16),
+        ),
+        in_specs=[pl.BlockSpec(memory_space=pl.ANY)] * 9,
+        out_specs=(pl.BlockSpec(memory_space=pltpu.VMEM),) * 2,
+        scratch_shapes=jax.tree.leaves(scratch_table()),
+        compiler_params=pltpu.CompilerParams(collective_id=0, has_side_effects=True, vmem_limit_bytes=40 * 2**20),
+    )(*operands)
     return moe, attention.reshape(1, 2, 2, QROWS // 2, VLAT)
 
 

time: 55.8 us -> 47 us (0.84)
  the two profiles are of different devices: /device:TPU:1 before, /device:TPU:33 now
where the time goes in v3:
time: 47 us; the launch traced here: 46.8 us
  Pallas kernels  44.8 us (95%)
  local copies, waits for them, and re-layouts  1.33 us (3%)
  between operations  0.64 us (1%)
    pallas_call x1, Pallas kernels, local(): pl.pallas_call(kernel, out_shape=(jax.ShapeDtypeStruct((TOK, WIDTH), BF16...  44.8 us
    unnamed x2, local copies, waits for them, and re-layouts  1.33 us

profile of v3, /device:TPU:33, one launch (start us, length us, event | category | flops | bytes accessed | tf_op | source)
XLA Modules:
  0.0 46.8 jit_solution(14828749030522173166)
XLA Ops:
  0.6 44.8 %shard_map.104 = (bf16[16,1792]{1,0:T(8,128)(2,1)S(1)}, bf16[256,512]{1,0:T(8,128)(2,1)S(1)}) custom-call(s32[8,16]{1,0:T(8,128)} %bitcast.16, f32[8,16]{1,0:T(8,128)} %bitcast.17, bf16[256,512]{1,0:T(8,128)(2,1)} %bitcast.14, bf16[1024,1792]{1,0:T(8,128)(2,1)} %bitcast.11, bf16[256,576]{1,0:T(8,128)(2,1)} %bitcast.13, bf16[2,2,576]{2,1,0:T(2,128)(2,1)} %bitcast.15, ...), custom_call_target="tpu_custom_call" | custom-call | tf_op jit(solution)/shard_map/pallas_call | solution.py:514
  45.5 0.6 %copy.13 = bf16[16,1792]{1,0:T(8,128)(2,1)} copy(bf16[16,1792]{1,0:T(8,128)(2,1)S(1)} %get-tuple-element.8) | data formatting | bytes 114688
  46.1 0.7 %copy.14 = bf16[1,2,2,64,512]{4,3,2,1,0:T(8,128)(2,1)} copy(bf16[1,2,2,64,512]{4,3,2,1,0:T(8,128)(2,1)S(1)} %bitcast.10) | data formatting | bytes 524288

commit v4 on v3

--- a/solution.py
+++ b/solution.py
@@ -30,6 +30,7 @@
 FAR = (5, -7, 7, -5, 8, 6, -6, 0)
 NEAR = (1, -3, 3, -1, 4, -4, 2, -2)
 HALVES = (FAR, NEAR)
+PARTS = ((0, 0, 5), (1, 0, 6), (0, 5, 8), (1, 6, 8))
 
 
 class Chunk:
@@ -54,7 +55,7 @@
         self.second_hops = (-2, 2) if near else (-6, 6)
 
 
-CHUNKS = tuple(Chunk(*each) for each in ((0, 0, 896), (0, 896, 896), (1, 0, 896), (1, 896, 896)))
+CHUNKS = tuple(Chunk(*each) for each in ((0, 0, 896), (0, 896, 896), (1, 0, 1152), (1, 1152, 640)))
 
 
 def remote(src, dst, send, recv, device):
@@ -199,15 +200,12 @@
 
     pl.semaphore_wait(barrier, 2 + LOW - 1 + 4)
 
-    for half, offsets in enumerate(HALVES):
-        for number, offset in enumerate(offsets):
-            remote(
-                hidden_hbm.at[plane_rows(offset)],
-                ref.hidden_in.at[half, pl.ds(number * TOK, TOK)],
-                ref.hidden_sem.at[0, half],
-                ref.hidden_sem.at[1, half],
-                partner,
-            ).start()
+    wait_for(ref.hidden, local.at[2])
+    for part, (half, first, last) in enumerate(PARTS):
+        place = (half, pl.ds(first * TOK, (last - first) * TOK))
+        remote(
+            ref.hidden.at[place], ref.hidden_in.at[place], ref.hidden_sem.at[0, part], ref.hidden_sem.at[1, part], partner
+        ).start()
     swap_copy = remote(
         queries_hbm.at[pl.ds(QROWS, QROWS)], ref.query_swap, ref.swap_sem.at[0], ref.swap_sem.at[1], sibling
     )
@@ -235,30 +233,40 @@
 
     own_units = pl.ds(pl.multiple_of(tp * HALF, HALF), HALF)
     other_units = pl.ds(pl.multiple_of((1 - tp) * HALF, HALF), HALF)
-    wait_for(ref.hidden, local.at[2])
     down_here.wait()
     for half in range(2):
         ref.first_half[half] = dot(ref.hidden[half], ref.down[own_units, :])
     pass_gates(1)
 
+    cache_copy = remote(ref.cache, ref.cache_in, ref.tp_sem.at[2], ref.tp_sem.at[3], partner)
+
+    def send_cache(section):
+        @pl.when(role == section)
+        def _():
+            cache_copy.start()
+
+    cache_here.wait()
     x_sem = ref.x_sem
-    for c, chunk in enumerate(CHUNKS):
-        half, columns, sent = chunk.half, chunk.columns, chunk.sent * TOK
-        if columns.start == 0:
-            if half == 1:
-                pass_gates(2)
-            wait_for(ref.hidden_in.at[half], ref.hidden_sem.at[1, half])
-        rows = ref.first_half[half, :, columns] + dot(ref.hidden_in[half], ref.down[other_units, columns])
-        rows = rows.astype(BF16)
-        ref.first_out[half, 0:sent, columns] = rows[:sent]
-        ref.first_in[half, sent:, columns] = rows[sent:]
-        for first, blocks, step in chunk.first_hops:
-            place = (half, pl.ds(first * TOK, blocks * TOK), columns)
-            remote(ref.first_out.at[place], ref.first_in.at[place], x_sem.at[0, c], x_sem.at[1, c], along_z(step)).start()
-
-    cache_here.wait()
-    cache_copy = remote(ref.cache, ref.cache_in, ref.tp_sem.at[2], ref.tp_sem.at[3], partner)
-    cache_copy.start()
+    for part, (half, first, last) in enumerate(PARTS):
+        place = pl.ds(first * TOK, (last - first) * TOK)
+        if part == 1:
+            pass_gates(2)
+        wait_for(ref.hidden_in.at[half, place], ref.hidden_sem.at[1, part])
+        if part == 3:
+            send_cache(0)
+        for c, chunk in enumerate(CHUNKS):
+            if chunk.half != half:
+                continue
+            columns = chunk.columns
+            rows = ref.first_half[half, place, columns] + dot(ref.hidden_in[half, place, :], ref.down[other_units, columns])
+            if part >= 2:
+                ref.first_in[half, place, columns] = rows.astype(BF16)
+                continue
+            ref.first_out[half, place, columns] = rows.astype(BF16)
+            for block, blocks, step in chunk.first_hops:
+                sent = (half, pl.ds(block * TOK, blocks * TOK), columns)
+                remote(ref.first_out.at[sent], ref.first_in.at[sent], x_sem.at[0, c], x_sem.at[1, c], along_z(step)).start()
+
     queries_here.wait()
     span_here.wait()
     latents = [ref.latents[group].astype(F32) for group in range(2)]
@@ -395,6 +403,7 @@
 
     exchange(0)
     exchange(1)
+    send_cache(1)
     pass_gates(3)
     for chunk in {chunk.kind: chunk for chunk in CHUNKS}.values():
         gate_matrix(chunk)
@@ -414,8 +423,8 @@
     for stage in range(3):
         for side in range(2):
             wait_for(ref.gates_out, ref.gate_sem.at[0, stage, side])
-    for half in range(2):
-        wait_for(ref.hidden_in.at[half], ref.hidden_sem.at[0, half])
+    for part, (half, first, last) in enumerate(PARTS):
+        wait_for(ref.hidden_in.at[half, pl.ds(first * TOK, (last - first) * TOK)], ref.hidden_sem.at[0, part])
     for c, chunk in enumerate(CHUNKS):
         half, columns = chunk.half, chunk.columns
         wait_for(ref.first_out.at[half, pl.ds(0, chunk.sent * TOK), columns], x_sem.at[0, c])
@@ -478,7 +487,7 @@
         swap_sem=dma((4,)),
         gate_sem=dma((2, 3, 2)),
         x_sem=dma((6, len(CHUNKS))),
-        hidden_sem=dma((2, 2)),
+        hidden_sem=dma((2, 4)),
     )
 
 

time: 47 us -> 45.3 us (0.964)
  the two profiles are of different devices: /device:TPU:33 before, /device:TPU:1 now
where the time goes in v4:
time: 45.3 us; the launch traced here: 45.1 us
  Pallas kernels  43.1 us (95%)
  local copies, waits for them, and re-layouts  1.33 us (3%)
  between operations  0.64 us (1%)
    pallas_call x1, Pallas kernels, local(): pl.pallas_call(kernel, out_shape=(jax.ShapeDtypeStruct((TOK, WIDTH), BF16...  43.1 us
    unnamed x2, local copies, waits for them, and re-layouts  1.33 us

profile of v4, /device:TPU:1, one launch (start us, length us, event | category | flops | bytes accessed | tf_op | source)
XLA Modules:
  0.0 45.1 jit_solution(6929756521151707297)
XLA Ops:
  0.6 43.1 %shard_map.104 = (bf16[16,1792]{1,0:T(8,128)(2,1)S(1)}, bf16[256,512]{1,0:T(8,128)(2,1)S(1)}) custom-call(s32[8,16]{1,0:T(8,128)} %bitcast.16, f32[8,16]{1,0:T(8,128)} %bitcast.17, bf16[256,512]{1,0:T(8,128)(2,1)} %bitcast.14, bf16[1024,1792]{1,0:T(8,128)(2,1)} %bitcast.11, bf16[256,576]{1,0:T(8,128)(2,1)} %bitcast.13, bf16[2,2,576]{2,1,0:T(2,128)(2,1)} %bitcast.15, ...), custom_call_target="tpu_custom_call" | custom-call | tf_op jit(solution)/shard_map/pallas_call | solution.py:523
  43.7 0.6 %copy.13 = bf16[16,1792]{1,0:T(8,128)(2,1)} copy(bf16[16,1792]{1,0:T(8,128)(2,1)S(1)} %get-tuple-element.8) | data formatting | bytes 114688
  44.4 0.7 %copy.14 = bf16[1,2,2,64,512]{4,3,2,1,0:T(8,128)(2,1)} copy(bf16[1,2,2,64,512]{4,3,2,1,0:T(8,128)(2,1)S(1)} %bitcast.10) | data formatting | bytes 524288

commit v5 on v4

--- a/solution.py
+++ b/solution.py
@@ -294,6 +294,7 @@
 
         @pl.loop(1, LOW)
         def _(step):
+            step = LOW - step
             rows_out = pl.ds(pl.multiple_of(step * TOK - TOK, TOK), TOK)
             rows_in = pl.ds(pl.multiple_of(step * TOK, TOK), TOK)
             remote(
@@ -353,10 +354,9 @@
     back_copy = remote(ref.answer_in, ref.answer_swap, ref.swap_sem.at[2], ref.swap_sem.at[3], sibling)
 
     def attend_first():
-        cache_copy.wait_recv()
-
         @pl.when(role == 0)
         def _():
+            cache_copy.wait_recv()
             ask_copy.wait_recv()
             top, total, value = scores_of(ref.query_in[...], keys, ref.span, length, tp, key_of < 4)
             ref.answer_out[:, :VLAT] = value.astype(BF16)
@@ -372,6 +372,10 @@
             answer_copy.start()
 
     def attend_own():
+        @pl.when(role == 1)
+        def _():
+            cache_copy.wait_recv()
+
         _, total, value = scores_of(ref.queries[:QROWS, :], keys, ref.span, length, tp, key_of <= step_of)
         attention_ref[:QROWS, :] = (value / total).astype(BF16)
 
@@ -414,8 +418,8 @@
     combine(2)
     combine(3)
     attend_first()
+    attend_back()
     attend_own()
-    attend_back()
     attend_last()
     finish()
 

time: 45.3 us -> 45.1 us (level)
  no operation moved by 1% of the time
where the time goes in v5:
time: 45.1 us; the launch traced here: 45 us
  Pallas kernels  43 us (95%)
  local copies, waits for them, and re-layouts  1.33 us (3%)
  between operations  0.64 us (1%)
    pallas_call x1, Pallas kernels, local(): pl.pallas_call(kernel, out_shape=(jax.ShapeDtypeStruct((TOK, WIDTH), BF16...  43 us
    unnamed x2, local copies, waits for them, and re-layouts  1.33 us

profile of v5, /device:TPU:1, one launch (start us, length us, event | category | flops | bytes accessed | tf_op | source)
XLA Modules:
  0.0 45.0 jit_solution(14886194020002425894)
XLA Ops:
  0.6 43.0 %shard_map.104 = (bf16[16,1792]{1,0:T(8,128)(2,1)S(1)}, bf16[256,512]{1,0:T(8,128)(2,1)S(1)}) custom-call(s32[8,16]{1,0:T(8,128)} %bitcast.16, f32[8,16]{1,0:T(8,128)} %bitcast.17, bf16[256,512]{1,0:T(8,128)(2,1)} %bitcast.14, bf16[1024,1792]{1,0:T(8,128)(2,1)} %bitcast.11, bf16[256,576]{1,0:T(8,128)(2,1)} %bitcast.13, bf16[2,2,576]{2,1,0:T(2,128)(2,1)} %bitcast.15, ...), custom_call_target="tpu_custom_call" | custom-call | tf_op jit(solution)/shard_map/pallas_call | solution.py:527
  43.6 0.6 %copy.13 = bf16[16,1792]{1,0:T(8,128)(2,1)} copy(bf16[16,1792]{1,0:T(8,128)(2,1)S(1)} %get-tuple-element.8) | data formatting | bytes 114688
  44.3 0.7 %copy.14 = bf16[1,2,2,64,512]{4,3,2,1,0:T(8,128)(2,1)} copy(bf16[1,2,2,64,512]{4,3,2,1,0:T(8,128)(2,1)S(1)} %bitcast.10) | data formatting | bytes 524288

commit v6 on v5

--- a/solution.py
+++ b/solution.py
@@ -178,7 +178,7 @@
     down_here = fetch(3, down_hbm, ref.down)
     cache_here = fetch(4, cache_hbm, ref.cache)
     queries_here = fetch(5, queries_hbm, ref.queries)
-    span_here = fetch(6, span_hbm, ref.latents)
+    span_here = fetch(6, span_hbm, ref.span)
     lengths_here = fetch(7, lengths_hbm, ref.lengths)
     destinations_here = fetch(8, destinations_hbm, ref.destinations)
 
@@ -269,8 +269,6 @@
 
     queries_here.wait()
     span_here.wait()
-    latents = [ref.latents[group].astype(F32) for group in range(2)]
-    ref.span[...] = jnp.concatenate(latents + [jnp.zeros((SPAN - 4, LAT), F32)], axis=0).astype(BF16)
     lengths_here.wait()
     destinations_here.wait()
     length = ref.lengths[role * 128 + ep]
@@ -470,7 +468,6 @@
         answer_out=pltpu.VMEM((QROWS, VLAT + 128), BF16),
         answer_in=pltpu.VMEM((QROWS, VLAT + 128), BF16),
         answer_swap=pltpu.VMEM((QROWS, VLAT + 128), BF16),
-        latents=pltpu.VMEM((2, 2, LAT), BF16),
         span=pltpu.VMEM((SPAN, LAT), BF16),
         lengths=pltpu.SMEM((256,), jnp.int32),
         destinations=pltpu.SMEM((128,), jnp.int32),
@@ -518,7 +515,7 @@
         expert_hidden[0],
         down_weight[0],
         queries.reshape(2 * QROWS, LAT),
-        new_latents[0],
+        jnp.pad(new_latents.reshape(4, LAT), ((0, SPAN - 4), (0, 0))),
         lengths,
         destinations,
         jnp.swapaxes(latent_cache[0], 0, 1),

time: 45.1 us -> 46.8 us (1.038)
  local copies, waits for them, and re-layouts: 1.33 us -> 2.65 us
    reshape x0 -> x1, local copies, waits for them, and re-layouts: none -> 0.71 us  [local(): new_latents.reshape(4, LAT)]
    pad x0 -> x1, local copies, waits for them, and re-layouts: none -> 0.62 us  [local(): jnp.pad(new_latents.reshape(4, LAT), ((0, SPAN - 4), (0, 0)))]
where the time goes in v6:
time: 46.8 us; the launch traced here: 46.6 us
  Pallas kernels  43.3 us (93%)
  local copies, waits for them, and re-layouts  2.65 us (6%)
  between operations  0.64 us (1%)
    pallas_call x1, Pallas kernels, local(): pl.pallas_call(kernel, out_shape=(jax.ShapeDtypeStruct((TOK, WIDTH), BF16...  43.3 us
    unnamed x2, local copies, waits for them, and re-layouts  1.33 us

profile of v6, /device:TPU:1, one launch (start us, length us, event | category | flops | bytes accessed | tf_op | source)
XLA Modules:
  0.0 46.6 jit_solution(5216063319955210207)
XLA Ops:
  0.6 0.7 %reshape.14 = bf16[4,576]{1,0:T(4,128)(2,1)S(1)} reshape(bf16[1,2,2,576]{3,2,1,0:T(2,128)(2,1)} %param.14) | data formatting | bytes 9216 | tf_op jit(solution)/shard_map/reshape | solution.py:518
  1.3 0.6 %pad.4.span_hbm = bf16[16,576]{1,0:T(8,128)(2,1)} pad(bf16[4,576]{1,0:T(4,128)(2,1)S(1)} %reshape.14, bf16[]{:T(256)} %constant.2.clone.1), padding=0_12x0_0 | pad | bytes 23042 | tf_op jit(solution)/shard_map/jit(_pad)/pad | solution.py:518
  2.0 43.3 %shard_map.104 = (bf16[16,1792]{1,0:T(8,128)(2,1)S(1)}, bf16[256,512]{1,0:T(8,128)(2,1)S(1)}) custom-call(s32[8,16]{1,0:T(8,128)} %bitcast.14, f32[8,16]{1,0:T(8,128)} %bitcast.15, bf16[256,512]{1,0:T(8,128)(2,1)} %bitcast.13, bf16[1024,1792]{1,0:T(8,128)(2,1)} %bitcast.10, bf16[256,576]{1,0:T(8,128)(2,1)} %bitcast.12, bf16[16,576]{1,0:T(8,128)(2,1)} %pad.4.span_hbm, ...), custom_call_target="tpu_custom_call" | custom-call | tf_op jit(solution)/shard_map/pallas_call | solution.py:524
  45.3 0.6 %copy.13 = bf16[16,1792]{1,0:T(8,128)(2,1)} copy(bf16[16,1792]{1,0:T(8,128)(2,1)S(1)} %get-tuple-element.8) | data formatting | bytes 114688
  45.9 0.7 %copy.14 = bf16[1,2,2,64,512]{4,3,2,1,0:T(8,128)(2,1)} copy(bf16[1,2,2,64,512]{4,3,2,1,0:T(8,128)(2,1)S(1)} %bitcast.9) | data formatting | bytes 524288
